TPU v7x, 32 devices: a whole 2x2x4 slice. The times are simulated.
32 devices in a mesh: img: 4 (over y, core), fsdp: 8 (over z, x).
Axes of the slice: x: 2, y: 2, z: 4, core: 2. Of those that a mesh axis runs over, the one named last changes fastest.
Arguments:
- text_states: bfloat16 [2048, 8192], P('img', 'fsdp'), may hold values from -100 to 100, as said below
- text_gain: float32 [8192], P('fsdp'), may hold values from 0.1 to 1.9
- gate_scale: float32 [8192], P('fsdp'), may hold values from 0.3 to 1.5
- live_counts: int32 [4], P('img'), may hold values from 1 to 512, 1536 in all
- token_slot: int32 [4, 512], P('img'), may hold values from 0 to 7, never falling along the last dimension, each value on 1 to 256 neighbouring positions
- wanted_images: int32 [4, 8], replicated, may hold values from 0 to 15, as said below
- patches: bfloat16 [16, 256, 1280], P('img', None, 'fsdp'), may hold values from -100 to 100, as said below
- latent_init: bfloat16 [64, 1280], replicated, may hold values from -100 to 100, as said below
- context_gain: float32 [1280], replicated, may hold values from 0.1 to 1.9
- latent_gain: float32 [1280], replicated, may hold values from 0.1 to 1.9
- res_query: bfloat16 [1280, 1536], P(None, 'fsdp'), may hold values from -0.15625 to 0.15625
- res_key: bfloat16 [1280, 1536], P(None, 'fsdp'), may hold values from -0.15625 to 0.15625
- res_value: bfloat16 [1280, 1536], P(None, 'fsdp'), may hold values from -0.15625 to 0.15625
- res_out: bfloat16 [1536, 1280], P('fsdp'), may hold values from -0.21875 to 0.21875
- final_gain: float32 [1280], P('fsdp'), may hold values from 0.1 to 1.9
- cross_query: bfloat16 [8192, 8192], P('fsdp'), may hold values from -0.09375 to 0.09375
- cross_key: bfloat16 [1280, 8192], P('fsdp'), may hold values from -0.25 to 0.25
- cross_value: bfloat16 [1280, 8192], P('fsdp'), may hold values from -0.25 to 0.25
- cross_out: bfloat16 [8192, 8192], P('fsdp'), may hold values from -0.09375 to 0.09375
Outputs:
- layer_output: float32 [2048, 8192], P('img', 'fsdp')
Inputs may be any that keep to these rules, and one draw needn't show every extreme that they name: `wanted_images`: image i is held by owner i // 4 along img. A row lists 8 distinct images; every owner that appears in a row has exactly 2 of its images there. `token_slot`: along a shard's tokens the slot never falls, and every slot of the shard is used. Tokens of shard s at positions live_counts[s] and beyond are padding. `text_states`: real values. `patches`: real values. `latent_init`: real values.
All inputs are finite; a program needn't handle non-finite values.
Results may differ from a plain program's by a relative error of at most 0.0075.
Values may be sent and summed in bfloat16 or wider, within the bound.
A program may use at most 128 MiB of HBM per device.

v0:
```python
import functools

import jax
import jax.numpy as jnp
from jax import lax
from jax.experimental import pallas as pl
from jax.experimental.pallas import tpu as pltpu
from jax.sharding import PartitionSpec as P

D = 8192
HEAD = 128
RHD = 96
PAIR = 2


eps_norm = 1e-05
eps_rms = 1e-06


def layer_norm(values, gain_vec):
    values = values.astype(jnp.float32)
    row_mean = jnp.mean(values, -1, keepdims=True)
    spread = jnp.mean(values * values, -1, keepdims=True) - row_mean * row_mean
    return (values - row_mean) * lax.rsqrt(spread + eps_norm) * gain_vec


def route_tables(wanted_images, per_owner, pair_slots):
    owners = wanted_images // per_owner
    slot_total = wanted_images.shape[1]
    positions = jnp.arange(slot_total, dtype=jnp.int32)
    before = (owners[:, :, None] == owners[:, None, :]) & (
        positions[None, None, :] < positions[None, :, None]
    )
    slot_rank = jnp.sum(before.astype(jnp.int32), axis=2)
    rank_hot = (
        slot_rank[:, :, None] == jnp.arange(pair_slots, dtype=jnp.int32)[None, None, :]
    ).astype(jnp.float32)
    return (owners, rank_hot)


def pack_rows(row_data, wanted_images, my_shard, per_owner, pair_slots):
    owners, rank_hot = route_tables(wanted_images, per_owner, pair_slots)
    is_mine = (owners == my_shard).astype(jnp.float32)
    local_hot = (
        (wanted_images % per_owner)[:, :, None]
        == jnp.arange(per_owner, dtype=jnp.int32)[None, None, :]
    ).astype(jnp.float32)
    picker = jnp.einsum("scp,sci->spi", rank_hot * is_mine[:, :, None], local_hot).astype(
        jnp.bfloat16
    )
    return jnp.einsum("spi,if->spf", picker, row_data, preferred_element_type=jnp.float32).astype(
        jnp.bfloat16
    )


def unpack_rows(received, wanted_images, my_shard, per_owner, pair_slots):
    owners, rank_hot = route_tables(wanted_images, per_owner, pair_slots)
    owner_row = lax.dynamic_slice_in_dim(owners, my_shard, 1, 0)[0]
    rank_row = lax.dynamic_slice_in_dim(rank_hot, my_shard, 1, 0)[0]
    source_hot = (
        owner_row[:, None] == jnp.arange(received.shape[0], dtype=jnp.int32)[None, :]
    ).astype(jnp.float32)
    taker = (source_hot[:, :, None] * rank_row[:, None, :]).astype(jnp.bfloat16)
    return jnp.einsum("cop,opf->cf", taker, received, preferred_element_type=jnp.float32).astype(
        jnp.bfloat16
    )


MESH = pl.DeviceIdType.MESH
LINE = 4
HALVES = 2
TILE = 256
LANES = 128
SPARE_ROWS = 2


def remote(src, dst, send, recv, target):
    return pltpu.make_async_remote_copy(
        src_ref=src,
        dst_ref=dst,
        send_sem=send,
        recv_sem=recv,
        device_id={"fsdp": target},
        device_id_type=MESH,
    )


def product_scatter_kernel(
    rows_ref, weight_ref, out_ref,
    weight, own, x_out, x_in, z_out, z_in,
    w_sem, x_send, x_recv, z_send, z_recv,
):
    me = lax.axis_index("fsdp")
    line, side = me // 2, me % 2
    across = line * 2 + (1 - side)
    is_end = (line == 0) | (line == LINE - 1)
    is_mid = jnp.logical_not(is_end)
    low = line < 2
    near_line = jnp.where(line % 2 == 0, line + 1, line - 1)
    near = near_line * 2 + side
    other_mid = (LINE - 1 - line) * 2 + side
    places = (
        jnp.where(low, 3, 0),
        jnp.where(low, 2, 1),
        near_line,
        line,
    )
    width = weight.shape[2]
    half = width // HALVES

    def fetch(slot):
        step, part = slot % LINE, slot // LINE
        block = places[step] * 2 + (side if part else 1 - side)
        return pltpu.make_async_copy(
            weight_ref.at[:, pl.ds(pl.multiple_of(block * width, width), width)],
            weight.at[slot],
            w_sem.at[slot],
        )

    for slot in range(2 * LINE):
        fetch(slot).start()

    barrier = pltpu.get_barrier_semaphore()
    for target in (across, near):
        pl.semaphore_signal(barrier, inc=1, device_id={"fsdp": target}, device_id_type=MESH)

    @pl.when(is_mid)
    def _():
        pl.semaphore_signal(barrier, inc=1, device_id={"fsdp": other_mid}, device_id_type=MESH)
        pl.semaphore_wait(barrier, 3)

    @pl.when(is_end)
    def _():
        pl.semaphore_wait(barrier, 2)

    def multiply(slot, into, step):
        for h in range(HALVES):

            def tile(c, carry, h=h):
                lower = pl.multiple_of(c * TILE, TILE)
                into[step, h, :, pl.ds(lower, TILE)] = jnp.dot(
                    rows_ref[...],
                    weight[slot, :, pl.ds(pl.multiple_of(h * half + lower, TILE), TILE)],
                    preferred_element_type=jnp.float32,
                ).astype(into.dtype)
                return carry

            lax.fori_loop(0, half // TILE, tile, 0)

    def x_copy(step, h):
        return remote(
            x_out.at[step, h], x_in.at[step, h], x_send.at[step, h], x_recv.at[step, h], across
        )

    def z_copy(step, h):
        if step < 2:
            slot, target = jnp.where(is_end, step, 3 + step), jnp.where(is_end, near, other_mid)
        else:
            slot, target = jnp.where(is_end, 2, 0), near
        return remote(
            z_out.at[step, h], z_in.at[slot, h], z_send.at[step, h], z_recv.at[slot, h], target
        )

    def z_arrived(slot, h):
        remote(
            z_out.at[0, h], z_in.at[slot, h], z_send.at[0, h], z_recv.at[slot, h], near
        ).wait_recv()

    for step in range(LINE):
        fetch(step).wait()
        multiply(step, x_out, step)
        for h in range(HALVES):
            x_copy(step, h).start()
    for step in range(LINE):
        fetch(LINE + step).wait()
        multiply(LINE + step, own, step)

    for step in range(LINE):
        for h in range(HALVES):
            x_copy(step, h).wait_recv()
            if step < LINE - 1:
                arriving = step if step < 2 else 3

                @pl.when(is_end)
                def _(step=step, h=h):
                    z_out[step, h] = (
                        own[step, h].astype(jnp.float32) + x_in[step, h].astype(jnp.float32)
                    ).astype(z_out.dtype)

                @pl.when(is_mid)
                def _(step=step, h=h, arriving=arriving):
                    z_arrived(arriving, h)
                    z_out[step, h] = (
                        own[step, h].astype(jnp.float32)
                        + x_in[step, h].astype(jnp.float32)
                        + z_in[arriving, h].astype(jnp.float32)
                    ).astype(z_out.dtype)

                z_copy(step, h).start()
            else:

                @pl.when(is_end)
                def _(step=step, h=h):
                    z_arrived(0, h)
                    out_ref[:, h * half : (h + 1) * half] = (
                        own[step, h].astype(jnp.float32)
                        + x_in[step, h].astype(jnp.float32)
                        + z_in[0, h].astype(jnp.float32)
                    )

                @pl.when(is_mid)
                def _(step=step, h=h):
                    z_arrived(2, h)
                    z_arrived(4, h)
                    out_ref[:, h * half : (h + 1) * half] = (
                        own[step, h].astype(jnp.float32)
                        + x_in[step, h].astype(jnp.float32)
                        + z_in[2, h].astype(jnp.float32)
                        + z_in[4, h].astype(jnp.float32)
                    )

    for step in range(LINE):
        for h in range(HALVES):
            x_copy(step, h).wait_send()
            if step < LINE - 1:
                z_copy(step, h).wait_send()


def product_scatter(rows, weight, collective_id):
    size = lax.axis_size("fsdp")
    if size != 2 * LINE:
        part = jnp.dot(rows, weight, preferred_element_type=jnp.float32).astype(jnp.bfloat16)
        return lax.psum_scatter(part, "fsdp", scatter_dimension=1, tiled=True).astype(jnp.float32)
    count, depth = rows.shape
    width = weight.shape[1] // size
    unit = (HALVES, count, width // HALVES)
    return pl.pallas_call(
        product_scatter_kernel,
        out_shape=jax.ShapeDtypeStruct((count, width), jnp.float32),
        in_specs=[
            pl.BlockSpec(memory_space=pltpu.VMEM),
            pl.BlockSpec(memory_space=pl.ANY),
        ],
        out_specs=pl.BlockSpec(memory_space=pltpu.VMEM),
        scratch_shapes=[
            pltpu.VMEM((2 * LINE, depth, width), jnp.bfloat16),
            pltpu.VMEM((LINE,) + unit, jnp.bfloat16),
            pltpu.VMEM((LINE,) + unit, jnp.bfloat16),
            pltpu.VMEM((LINE,) + unit, jnp.bfloat16),
            pltpu.VMEM((LINE - 1,) + unit, jnp.bfloat16),
            pltpu.VMEM((LINE + 1,) + unit, jnp.bfloat16),
            pltpu.SemaphoreType.DMA((2 * LINE,)),
            pltpu.SemaphoreType.DMA((LINE, HALVES)),
            pltpu.SemaphoreType.DMA((LINE, HALVES)),
            pltpu.SemaphoreType.DMA((LINE - 1, HALVES)),
            pltpu.SemaphoreType.DMA((LINE + 1, HALVES)),
        ],
        compiler_params=pltpu.CompilerParams(
            collective_id=collective_id,
            has_side_effects=True,
            vmem_limit_bytes=50 * 1024 * 1024,
        ),
        cost_estimate=pl.CostEstimate(
            flops=2 * count * depth * width * size,
            bytes_accessed=300_000_000,
            transcendentals=0,
        ),
        name="product_scatter",
    )(rows, weight)


def latents_kernel(
    part_ref, init_ref, stats_ref, rows_ref, sums_ref,
    part_in, rows_out, rows_in, stats_in,
    part_send, part_recv, rows_send, rows_recv, stats_send, stats_recv,
):
    me = lax.axis_index("fsdp")
    size = part_in.shape[0] + 1
    count = init_ref.shape[0]
    peers = [lax.rem(me + step, size) for step in range(1, size)]
    owners = [lax.rem(me + size - step, size) for step in range(1, size)]

    barrier = pltpu.get_barrier_semaphore()
    for target in peers:
        pl.semaphore_signal(barrier, inc=1, device_id={"fsdp": target}, device_id_type=MESH)
    pl.semaphore_wait(barrier, size - 1)

    def block(owner):
        return pl.ds(pl.multiple_of(owner * count, count), count)

    def stats_copy(i):
        return remote(stats_ref, stats_in.at[i], stats_send.at[i], stats_recv.at[i], peers[i])

    def part_copy(i):
        return remote(
            part_ref.at[block(peers[i]), :], part_in.at[i], part_send.at[i], part_recv.at[i],
            peers[i],
        )

    def rows_copy(i):
        return remote(rows_out, rows_in.at[i], rows_send.at[i], rows_recv.at[i], peers[i])

    for i in range(size - 1):
        part_copy(i).start()
        stats_copy(i).start()
    total = init_ref[...] + part_ref[block(me), :].astype(jnp.float32)
    sums = stats_ref[...]
    for i in range(size - 1):
        part_copy(i).wait_recv()
        stats_copy(i).wait_recv()
        total = total + part_in[i].astype(jnp.float32)
        sums = sums + stats_in[i]
    sums_ref[...] = sums
    first = sums.shape[0] - SPARE_ROWS - total.shape[1] // LANES
    gain = jnp.concatenate(
        [sums[first + r : first + r + 1, :] for r in range(total.shape[1] // LANES)], axis=1
    )
    rows_out[...] = layer_norm(total, gain).astype(rows_out.dtype)
    for i in range(size - 1):
        rows_copy(i).start()
    rows_ref[block(me), :] = rows_out[...]
    for i in range(size - 1):
        rows_copy(i).wait_recv()
        rows_ref[block(owners[i]), :] = rows_in[i]
    for i in range(size - 1):
        part_copy(i).wait_send()
        stats_copy(i).wait_send()
        rows_copy(i).wait_send()


def normed_latents(part, init_rows, stats):
    others = lax.axis_size("fsdp") - 1
    count, width = init_rows.shape
    return pl.pallas_call(
        latents_kernel,
        out_shape=(
            jax.ShapeDtypeStruct(part.shape, jnp.bfloat16),
            jax.ShapeDtypeStruct(stats.shape, jnp.float32),
        ),
        in_specs=[pl.BlockSpec(memory_space=pltpu.VMEM)] * 3,
        out_specs=(pl.BlockSpec(memory_space=pltpu.VMEM),) * 2,
        scratch_shapes=[
            pltpu.VMEM((others, count, width), jnp.bfloat16),
            pltpu.VMEM((count, width), jnp.bfloat16),
            pltpu.VMEM((others, count, width), jnp.bfloat16),
            pltpu.VMEM((others,) + stats.shape, jnp.float32),
        ]
        + [pltpu.SemaphoreType.DMA((others,))] * 6,
        compiler_params=pltpu.CompilerParams(
            collective_id=2, has_side_effects=True, vmem_limit_bytes=16 * 1024 * 1024
        ),
        cost_estimate=pl.CostEstimate(
            flops=part.size * 20, bytes_accessed=100_000_000, transcendentals=0
        ),
        name="normed_latents",
    )(part, init_rows, stats)


def pick_kernel(shard_ref, key_ref, value_ref, out_ref):
    width = key_ref.shape[1]
    out_ref[0, :, :width] = key_ref[...]
    out_ref[0, :, width:] = value_ref[...]


def pick_columns(cross_key, cross_value, parts, stride, part):
    rows = cross_key.shape[0]
    column = pl.BlockSpec((rows, part), lambda b, shard: (0, b * stride + shard[0]))
    return pl.pallas_call(
        pick_kernel,
        out_shape=jax.ShapeDtypeStruct((parts, rows, 2 * part), cross_key.dtype),
        grid_spec=pltpu.PrefetchScalarGridSpec(
            num_scalar_prefetch=1,
            grid=(parts,),
            in_specs=[column, column],
            out_specs=pl.BlockSpec((1, rows, 2 * part), lambda b, shard: (b, 0, 0)),
        ),
        name="pick_columns",
    )(lax.axis_index("img").astype(jnp.int32).reshape(1), cross_key, cross_value)


def head_weights(cross_key, cross_value):
    fsdp_size, img_size = lax.axis_size("fsdp"), lax.axis_size("img")
    my_shard = lax.axis_index("img")
    rows = cross_key.shape[0]
    part = cross_key.shape[1] // (fsdp_size * img_size)

    def mine(weight):
        split = weight.reshape(rows, fsdp_size, img_size, part)
        return lax.dynamic_index_in_dim(split, my_shard, 2, keepdims=False)

    if part % LANES == 0:
        both = pick_columns(cross_key, cross_value, fsdp_size, img_size, part)
    else:
        both = jnp.concatenate([mine(cross_key), mine(cross_value)], 2)
        both = jnp.transpose(both, (1, 0, 2))
    both = lax.all_to_all(both, "fsdp", split_axis=0, concat_axis=0, tiled=True)
    return lax.all_gather(both.reshape(fsdp_size * rows, 2 * part), "img", axis=0)


def local(
    text_states,
    text_gain,
    gate_scale,
    live_counts,
    token_slot,
    wanted_images,
    patches,
    latent_init,
    context_gain,
    latent_gain,
    res_query,
    res_key,
    res_value,
    res_out,
    final_gain,
    cross_query,
    cross_key,
    cross_value,
    cross_out,
):
    my_feature = lax.axis_index("fsdp")
    my_shard = lax.axis_index("img")
    image_count = patches.shape[0]
    patch_count = patches.shape[1]
    feat_vis = patches.shape[2]
    latent_count = latent_init.shape[0]
    vis_width = latent_init.shape[1]
    res_cols = res_query.shape[1]
    res_heads = res_cols // RHD
    head_cols = cross_out.shape[0]
    token_count = text_states.shape[0]
    slot_count = wanted_images.shape[1]
    cross_heads = head_cols // HEAD
    text_f = text_states.astype(jnp.float32)
    full_patches = lax.all_gather(patches, "fsdp", axis=2, tiled=True)
    gain_rows = lax.dynamic_update_slice_in_dim(
        jnp.zeros((vis_width,), jnp.float32), final_gain, my_feature * feat_vis, 0
    )
    stats = jnp.concatenate(
        [jnp.sum(text_f * text_f, -1), gain_rows, jnp.zeros((SPARE_ROWS * LANES,), jnp.float32)]
    ).reshape(-1, LANES)
    kv_weights = head_weights(cross_key, cross_value)
    query = product_scatter((text_f * text_gain).astype(jnp.bfloat16), cross_query, 0)
    full_patches, query = lax.optimization_barrier((full_patches, query))
    context = layer_norm(full_patches, context_gain).astype(jnp.bfloat16)
    latent_normed = layer_norm(latent_init, latent_gain).astype(jnp.bfloat16)
    res_q_rows = jnp.dot(latent_normed, res_query, preferred_element_type=jnp.float32).astype(
        jnp.bfloat16
    )
    res_q_rows = res_q_rows.reshape(latent_count, res_heads, RHD)
    ctx_keys = jnp.einsum(
        "npv,vk->npk", context, res_key, preferred_element_type=jnp.float32
    ).astype(jnp.bfloat16)
    ctx_values = jnp.einsum(
        "npv,vk->npk", context, res_value, preferred_element_type=jnp.float32
    ).astype(jnp.bfloat16)
    lat_keys = jnp.dot(latent_normed, res_key, preferred_element_type=jnp.float32).astype(
        jnp.bfloat16
    )
    lat_values = jnp.dot(latent_normed, res_value, preferred_element_type=jnp.float32).astype(
        jnp.bfloat16
    )
    joined_shape = (image_count, latent_count, res_cols)
    key_rows = jnp.concatenate([ctx_keys, jnp.broadcast_to(lat_keys[None], joined_shape)], 1)
    value_rows = jnp.concatenate([ctx_values, jnp.broadcast_to(lat_values[None], joined_shape)], 1)
    key_rows = key_rows.reshape(image_count, patch_count + latent_count, res_heads, RHD)
    value_rows = value_rows.reshape(image_count, patch_count + latent_count, res_heads, RHD)
    res_scores = jnp.einsum(
        "rhe,nkhe->nhrk", res_q_rows, key_rows, preferred_element_type=jnp.float32
    ) * RHD ** (-0.5)
    res_weights = jnp.exp(res_scores)
    res_weights = (res_weights / jnp.sum(res_weights, -1, keepdims=True)).astype(jnp.bfloat16)
    res_mixed = jnp.einsum(
        "nhrk,nkhe->nrhe", res_weights, value_rows, preferred_element_type=jnp.float32
    )
    res_mixed = res_mixed.astype(jnp.bfloat16).reshape(image_count * latent_count, res_cols)
    mixed_part = jnp.dot(res_mixed, res_out, preferred_element_type=jnp.float32)
    row_count = mixed_part.shape[0] // lax.axis_size("fsdp")
    init_rows = lax.dynamic_slice_in_dim(
        latent_init, (my_feature * row_count) % latent_count, row_count, 0
    ).astype(jnp.float32)
    resampled, sums = normed_latents(mixed_part.astype(jnp.bfloat16), init_rows, stats)
    squares = sums.reshape(-1)[:token_count]
    query = (query * lax.rsqrt(squares / D + eps_rms)[:, None]).astype(jnp.bfloat16)
    per_image = resampled.reshape(image_count, latent_count * vis_width)
    outgoing = pack_rows(per_image, wanted_images, my_shard, image_count, PAIR)
    incoming = lax.all_to_all(outgoing, "img", split_axis=0, concat_axis=0, tiled=True)
    slot_latents = unpack_rows(incoming, wanted_images, my_shard, image_count, PAIR).reshape(
        slot_count * latent_count, vis_width
    )
    slot_kv = jnp.einsum(
        "lv,ivk->ilk", slot_latents, kv_weights, preferred_element_type=jnp.float32
    ).astype(jnp.bfloat16)
    slot_kv = slot_kv.reshape(kv_weights.shape[0], slot_count * latent_count, 2, -1)
    slot_kv = jnp.transpose(slot_kv, (2, 0, 3, 1)).reshape(2, cross_heads, HEAD, -1)
    slot_keys, slot_values = slot_kv[0], slot_kv[1]
    query_heads = jnp.transpose(query.reshape(token_count, cross_heads, HEAD), (1, 0, 2))
    scores = jnp.einsum(
        "hte,hel->htl", query_heads, slot_keys, preferred_element_type=jnp.float32
    ) * HEAD ** (-0.5)
    key_slot = jnp.arange(slot_count * latent_count, dtype=jnp.int32) // latent_count
    slot_hot = (token_slot[0][:, None] == key_slot[None, :]).astype(jnp.float32)
    weights = jnp.exp(scores) * slot_hot[None]
    weights = (weights / jnp.sum(weights, axis=2, keepdims=True)).astype(jnp.bfloat16)
    attended = jnp.einsum("htl,hel->the", weights, slot_values, preferred_element_type=jnp.float32)
    attended = attended.astype(jnp.bfloat16).reshape(token_count, head_cols)
    projected = product_scatter(attended, cross_out, 1)
    positions = jnp.arange(token_count, dtype=jnp.int32)
    live_mask = (positions < live_counts[0]).astype(jnp.float32)[:, None]
    return text_f + jnp.tanh(gate_scale) * projected * live_mask


def solution(mesh):
    placed = (
        P("img", "fsdp"),
        P("fsdp"),
        P("fsdp"),
        P("img"),
        P("img", None),
        P(),
        P("img", None, "fsdp"),
        P(),
        P(),
        P(),
        P(None, "fsdp"),
        P(None, "fsdp"),
        P(None, "fsdp"),
        P("fsdp", None),
        P("fsdp"),
        P("fsdp", None),
        P("fsdp", None),
        P("fsdp", None),
        P("fsdp", None),
    )
    return jax.shard_map(
        local, mesh=mesh, in_specs=placed, out_specs=P("img", "fsdp"), check_vma=False
    )
```

profile of v0, /device:TPU:0, one launch (start us, length us, event | category | flops | bytes accessed | tf_op | source)
XLA Modules:
  0.0 367.8 jit_solution(14596657873461003110)
XLA Ops:
  6.5 0.0 copy-start
  6.5 0.0 all-gather.5.cloned.1.call-start
  6.5 0.7 all-gather.5.cloned.1.call-update
  7.3 0.0 all-gather.3.cloned.1.call-start
  7.3 5.4 %pick_columns.1 = bf16[8,160,512]{2,1,0:T(8,128)(2,1)} custom-call(s32[1]{0:T(128)} %bitcast.shard_ref, bf16[160,8192]{1,0:T(8,128)(2,1)} %key_ref.1, bf16[160,8192]{1,0:T(8,128)(2,1)} %value_ref.1), custom_call_target="tpu_custom_call" | custom-call | tf_op jit(solution)/shard_map/pick_columns/pallas_call | solution.py:368
  12.7 0.0 copy-start.12
  12.7 61.9 %all_to_all.10 = bf16[8,160,512]{2,1,0:T(8,128)(2,1)} all-to-all(bf16[8,160,512]{2,1,0:T(8,128)(2,1)} %pick_columns.1), channel_id=1, replica_groups=mesh['img'=4,'fsdp'=8] {'fsdp'}, dimensions={0} | all-to-all | bytes 2621440 | tf_op jit(solution)/shard_map/all_to_all | solution.py:396
  74.6 0.0 copy-start.8
  74.6 0.0 all-gather.3.cloned.1.call-update
  74.6 0.0 copy-done.6
  74.6 0.1 convert_reduce_fusion.1
  74.8 0.0 copy-done.13
  74.8 0.0 copy-done.16
  74.8 0.3 convolution_convert_fusion.8
  75.1 0.1 copy.63
  75.2 1.4 convolution_convert_fusion.7
  76.6 0.1 copy.65
  76.7 0.0 copy-done.12
  76.7 0.3 convolution_convert_fusion.6
  77.0 0.1 reshape.192
  77.8 0.0 copy-done.9
  77.8 0.0 copy-done.11
  77.9 0.3 dynamic_update_slice.3
  78.1 0.0 copy-done.7
  78.2 0.2 convert_reduce_fusion.2
  78.4 0.4 fusion.8
  78.8 0.1 convolution_convert_fusion.9
  79.0 0.0 copy-start.14
  79.0 93.2 %product_scatter.2 = f32[512,1024]{1,0:T(8,128)S(1)} custom-call(bf16[512,1024]{1,0:T(8,128)(2,1)S(1)} %get-tuple-element.22.rows_ref, bf16[1024,8192]{1,0:T(8,128)(2,1)} %weight_ref.2), custom_call_target="tpu_custom_call" | custom-call | flops 8589934592 | bytes 300000000 | tf_op jit(solution)/shard_map/product_scatter/pallas_call | solution.py:237
  172.2 0.0 copy-start.17
  172.2 0.0 all-gather.5.cloned.1.call-done
  172.2 2.6 convert_reduce_fusion
  174.9 0.0 copy-start.15
  174.9 1.1 convolution_convert_fusion.4
  176.1 0.1 pad_maximum_fusion
  176.1 0.0 copy-done.15
  176.1 1.2 convolution_convert_fusion.3
  177.3 0.9 pad_maximum_fusion.1
  178.2 2.2 divide_convert_fusion.4
  180.4 1.4 fusion.13
  181.8 0.1 copy.69
  181.9 0.1 reshape.193
  182.1 0.3 convolution_convert_fusion.1.part_ref
  182.4 31.0 %normed_latents.1 = (bf16[256,1280]{1,0:T(8,128)(2,1)S(1)}, f32[16,128]{1,0:T(8,128)S(1)}) custom-call(bf16[256,1280]{1,0:T(8,128)(2,1)S(1)} %convolution_convert_fusion.1.part_ref, f32[32,1280]{1,0:T(8,128)S(1)} %dynamic-slice_convert_fusion.init_ref, f32[16,128]{1,0:T(8,128)S(1)} %maximum_bitcast_fusion.stats_ref), custom_call_target="tpu_custom_call" | custom-call | flops 6553600 | bytes 100000000 | tf_op jit(solution)/shard_map/normed_latents/pallas_call | solution.py:334
  213.5 1.3 reshape.203
  214.8 1.7 convolution_convert_fusion
  216.4 0.0 copy-start.10
  216.4 2.4 copy.71
  218.9 4.5 %all-to-all-start.1 = ((bf16[4,2,81920]{2,1,0:T(2,128)(2,1)}), bf16[4,2,81920]{2,1,0:T(2,128)(2,1)}, u32[]{:S(2)}, u32[]{:S(2)}) async-start(bf16[4,2,81920]{2,1,0:T(2,128)(2,1)} %copy.71), calls=%async_computation.1 | async-start | bytes 2621440 | tf_op jit(solution)/shard_map/all_to_all | solution.py:487
  223.5 1.1 compare_convert_fusion
  224.6 15.9 %all-to-all-done.1 = bf16[4,2,81920]{2,1,0:T(2,128)(2,1)} async-done(((bf16[4,2,81920]{2,1,0:T(2,128)(2,1)}), bf16[4,2,81920]{2,1,0:T(2,128)(2,1)}, u32[]{:S(2)}, u32[]{:S(2)}) %all-to-all-start.1) | async-done | bytes 1310752 | tf_op jit(solution)/shard_map/all_to_all | solution.py:487
  240.5 3.9 %fusion = bf16[8,81920]{1,0:T(8,128)(2,1)} fusion(bf16[4,2,81920]{2,1,0:T(2,128)(2,1)} %all-to-all-done.1, f32[8,2]{0,1:T(2,128)S(1)} %fusion.46, f32[8,4]{0,1:T(4,128)S(1)} %fusion.44), kind=kOutput, calls=%fused_computation.1 | convolution fusion | flops 11141248 | bytes 2621632 | tf_op jit(solution)/shard_map/cop,opf->cf/dot_general | solution.py:64
  244.4 3.0 reshape.205
  247.4 5.8 %convolution_convert_fusion.2 = bf16[4,512,512]{2,1,0:T(8,128)(2,1)S(1)} fusion(bf16[4,1280,512]{2,1,0:T(8,128)(2,1)} %all-gather.3.cloned.1.call-done, bf16[512,1280,1]{1,0,2:T(8,128)(2,1)} %reshape.205), kind=kOutput, calls=%fused_computation.22 | convolution fusion | flops 2685403136 | bytes 8650752 | tf_op jit(solution)/shard_map/lv,ivk->ilk/dot_general | solution.py:491
  253.2 0.2 copy.114
  253.5 0.1 fusion.59
  253.6 1.1 copy-done.4
  254.7 2.6 fusion.1
  257.3 2.2 fusion.9
  259.4 0.5 copy.87.rows_ref
  260.0 0.0 copy-start.3
  260.0 0.0 copy-start.1
  260.0 99.2 %product_scatter.3 = f32[512,1024]{1,0:T(8,128)S(1)} custom-call(bf16[512,1024]{1,0:T(8,128)(2,1)S(1)} %copy.87.rows_ref, bf16[1024,8192]{1,0:T(8,128)(2,1)} %weight_ref.3), custom_call_target="tpu_custom_call" | custom-call | flops 8589934592 | bytes 300000000 | tf_op jit(solution)/shard_map/product_scatter/pallas_call | solution.py:237
  359.3 1.7 convert_add_fusion
  (38 shorter events, 0.2 us)
Async XLA Ops:
  6.5 175.5 %copy-start = (bf16[192,1280]{1,0:T(8,128)(2,1)S(1)}, bf16[192,1280]{1,0:T(8,128)(2,1)}, u32[]{:S(2)}) copy-start(bf16[192,1280]{1,0:T(8,128)(2,1)} %param.32) | copy-start | bytes 1474564
  6.5 165.7 %all-gather.5.cloned.1.call-start = ((), (), s32[]{:S(2)}) async-start(), calls=%async_computation.3 | async-start | bytes 2949120 | tf_op jit(solution)/shard_map/all_gather | solution.py:435
  7.3 240.1 %all-gather.3.cloned.1.call-start = ((), (), s32[]{:S(2)}) async-start(), calls=%async_computation.2 | async-start | bytes 6553600 | tf_op jit(solution)/shard_map/all_gather | solution.py:397
  12.7 61.9 %copy-start.6 = (bf16[64,1280]{1,0:T(8,128)(2,1)S(1)}, bf16[64,1280]{1,0:T(8,128)(2,1)}, u32[]{:S(2)}) copy-start(bf16[64,1280]{1,0:T(8,128)(2,1)} %param.26) | copy-start | bytes 491524
  12.7 62.1 %copy-start.13 = (bf16[1280,192]{0,1:T(8,128)(2,1)S(1)}, bf16[1280,192]{0,1:T(8,128)(2,1)}, u32[]{:S(2)}) copy-start(bf16[1280,192]{0,1:T(8,128)(2,1)} %param.31) | copy-start | bytes 1474564
  12.7 62.1 %copy-start.16 = (f32[1280]{0:T(1024)S(1)}, f32[1280]{0:T(1024)}, u32[]{:S(2)}) copy-start(f32[1280]{0:T(1024)} %param.28) | copy-start | bytes 15364
  12.7 64.0 %copy-start.12 = (bf16[1280,192]{0,1:T(8,128)(2,1)S(1)}, bf16[1280,192]{0,1:T(8,128)(2,1)}, u32[]{:S(2)}) copy-start(bf16[1280,192]{0,1:T(8,128)(2,1)} %param.29) | copy-start | bytes 1474564
  74.6 3.3 copy-start.9
  74.6 3.3 copy-start.11
  74.6 3.6 copy-start.7
  74.6 3.8 %copy-start.2 = (bf16[512,1024]{1,0:T(8,128)(2,1)S(1)}, bf16[512,1024]{1,0:T(8,128)(2,1)}, u32[]{:S(2)}) copy-start(bf16[512,1024]{1,0:T(8,128)(2,1)} %param.19) | copy-start | bytes 3145732
  74.6 3.9 %copy-start.8 = (f32[1024]{0:T(1024)S(1)}, f32[1024]{0:T(1024)}, u32[]{:S(2)}) copy-start(f32[1024]{0:T(1024)} %param.20) | copy-start | bytes 12292
  79.0 95.8 %copy-start.14 = (bf16[1280,192]{0,1:T(8,128)(2,1)S(1)}, bf16[1280,192]{0,1:T(8,128)(2,1)}, u32[]{:S(2)}) copy-start(bf16[1280,192]{0,1:T(8,128)(2,1)} %param.31) | copy-start | bytes 1474564
  172.2 2.7 copy-start.17
  172.2 2.6 copy-start.5
  174.9 1.3 copy-start.15
  216.4 7.0 %copy-start.10 = (s32[1,512]{1,0:T(1,128)S(1)}, s32[1,512]{1,0:T(1,128)}, u32[]{:S(2)}) copy-start(s32[1,512]{1,0:T(1,128)} %param.23) | copy-start | bytes 6148
  218.9 21.7 %all-to-all-start.1 = ((bf16[4,2,81920]{2,1,0:T(2,128)(2,1)}), bf16[4,2,81920]{2,1,0:T(2,128)(2,1)}, u32[]{:S(2)}, u32[]{:S(2)}) async-start(bf16[4,2,81920]{2,1,0:T(2,128)(2,1)} %copy.71), calls=%async_computation.1 | async-start | bytes 2621440 | tf_op jit(solution)/shard_map/all_to_all | solution.py:487
  253.5 1.2 copy-start.4
  260.0 99.3 %copy-start.3 = (bf16[512,1024]{1,0:T(8,128)(2,1)S(1)}, bf16[512,1024]{1,0:T(8,128)(2,1)}, u32[]{:S(2)}) copy-start(bf16[512,1024]{1,0:T(8,128)(2,1)} %param.19) | copy-start | bytes 3145732
  260.0 101.0 %copy-start.1 = (bf16[192,1280]{1,0:T(8,128)(2,1)S(1)}, bf16[192,1280]{1,0:T(8,128)(2,1)}, u32[]{:S(2)}) copy-start(bf16[192,1280]{1,0:T(8,128)(2,1)} %param.32) | copy-start | bytes 1474564
Sparse Core Ops, SparseCore 0:
  9.6 73.9 all-gather.4
  85.1 39.5 all-gather.2
where the time goes:
time: 369 us; the launch traced here: 368 us
  Pallas kernels  229 us (62%)
  blocking collectives  61.9 us (17%)
  matrix products  24.4 us (7%)
  waiting for transfers between devices  16.7 us (5%)
  between operations  14.6 us (4%)
  local copies, waits for them, and re-layouts  9.73 us (3%)
  other arithmetic  7.18 us (2%)
  starting transfers between devices  4.57 us (1%)
    pallas_call x2, Pallas kernels, product_scatter(): pl.pallas_call(product_scatter_kernel, out_shape=jax.ShapeDtypeStruct((co...  192 us
    all_to_all x1, blocking collectives, head_weights(): both = lax.all_to_all(both, 'fsdp', split_axis=0, concat_axis=0, tiled=True)  61.9 us
    pallas_call x1, Pallas kernels, normed_latents(): pl.pallas_call(latents_kernel, out_shape=(jax.ShapeDtypeStruct(part.shape...  31 us
    all_to_all x1, waiting for transfers between devices, local(): lax.all_to_all(outgoing, 'img', split_axis=0, concat_axis=0, tiled=True)  15.9 us
  transfers between devices with their start and end apart: 3, of which 1 were waited for; matrix products, arithmetic and copies ran while one was open for 7% of the time, Pallas kernels for 35%

commit v1 on v0

--- a/solution.py
+++ b/solution.py
@@ -48,22 +48,22 @@
     picker = jnp.einsum("scp,sci->spi", rank_hot * is_mine[:, :, None], local_hot).astype(
         jnp.bfloat16
     )
-    return jnp.einsum("spi,if->spf", picker, row_data, preferred_element_type=jnp.float32).astype(
-        jnp.bfloat16
-    )
-
-
-def unpack_rows(received, wanted_images, my_shard, per_owner, pair_slots):
+    picked = picker[:, :, 0, None, None] * row_data[0]
+    for image in range(1, per_owner):
+        picked = picked + picker[:, :, image, None, None] * row_data[image]
+    return picked
+
+
+def arrived_slots(wanted_images, my_shard, per_owner, pair_slots):
     owners, rank_hot = route_tables(wanted_images, per_owner, pair_slots)
     owner_row = lax.dynamic_slice_in_dim(owners, my_shard, 1, 0)[0]
-    rank_row = lax.dynamic_slice_in_dim(rank_hot, my_shard, 1, 0)[0]
+    rank_row = lax.dynamic_slice_in_dim(rank_hot, my_shard, 1, 0)[0].astype(jnp.int32)
+    shards, slot_total = wanted_images.shape
     source_hot = (
-        owner_row[:, None] == jnp.arange(received.shape[0], dtype=jnp.int32)[None, :]
-    ).astype(jnp.float32)
-    taker = (source_hot[:, :, None] * rank_row[:, None, :]).astype(jnp.bfloat16)
-    return jnp.einsum("cop,opf->cf", taker, received, preferred_element_type=jnp.float32).astype(
-        jnp.bfloat16
-    )
+        owner_row[:, None] == jnp.arange(shards, dtype=jnp.int32)[None, :]
+    ).astype(jnp.int32)
+    numbered = jnp.arange(1, slot_total + 1, dtype=jnp.int32)[:, None, None]
+    return jnp.sum(source_hot[:, :, None] * rank_row[:, None, :] * numbered, 0) - 1
 
 
 MESH = pl.DeviceIdType.MESH
@@ -85,12 +85,15 @@
     )
 
 
-def product_scatter_kernel(
-    rows_ref, weight_ref, out_ref,
-    weight, own, x_out, x_in, z_out, z_in,
-    w_sem, x_send, x_recv, z_send, z_recv,
-):
+def product_scatter_kernel(exchange, *refs):
+    if exchange:
+        rows_ref, weight_ref, moved_ref, out_ref, moved_out, *refs = refs
+        *refs, moved_in, moved_send, moved_recv = refs
+    else:
+        rows_ref, weight_ref, out_ref, *refs = refs
+    weight, own, x_out, x_in, z_out, z_in, w_sem, x_send, x_recv, z_send, z_recv = refs
     me = lax.axis_index("fsdp")
+    size = 2 * LINE
     line, side = me // 2, me % 2
     across = line * 2 + (1 - side)
     is_end = (line == 0) | (line == LINE - 1)
@@ -121,17 +124,30 @@
         fetch(slot).start()
 
     barrier = pltpu.get_barrier_semaphore()
-    for target in (across, near):
-        pl.semaphore_signal(barrier, inc=1, device_id={"fsdp": target}, device_id_type=MESH)
-
-    @pl.when(is_mid)
-    def _():
-        pl.semaphore_signal(barrier, inc=1, device_id={"fsdp": other_mid}, device_id_type=MESH)
-        pl.semaphore_wait(barrier, 3)
-
-    @pl.when(is_end)
-    def _():
-        pl.semaphore_wait(barrier, 2)
+    if exchange:
+        for step in range(1, size):
+            pl.semaphore_signal(
+                barrier, inc=1, device_id={"fsdp": (me + step) % size}, device_id_type=MESH
+            )
+        pl.semaphore_wait(barrier, size - 1)
+    else:
+        for target in (across, near):
+            pl.semaphore_signal(barrier, inc=1, device_id={"fsdp": target}, device_id_type=MESH)
+
+        @pl.when(is_mid)
+        def _():
+            pl.semaphore_signal(barrier, inc=1, device_id={"fsdp": other_mid}, device_id_type=MESH)
+            pl.semaphore_wait(barrier, 3)
+
+        @pl.when(is_end)
+        def _():
+            pl.semaphore_wait(barrier, 2)
+
+    def moved_copy(i):
+        target = (me + i + 1) % size
+        return remote(
+            moved_ref.at[target], moved_in.at[i], moved_send.at[i], moved_recv.at[i], target
+        )
 
     def multiply(slot, into, step):
         for h in range(HALVES):
@@ -171,6 +187,9 @@
         multiply(step, x_out, step)
         for h in range(HALVES):
             x_copy(step, h).start()
+    if exchange:
+        for i in range(size - 1):
+            moved_copy(i).start()
     for step in range(LINE):
         fetch(LINE + step).wait()
         multiply(LINE + step, own, step)
@@ -219,6 +238,12 @@
                         + z_in[4, h].astype(jnp.float32)
                     )
 
+    if exchange:
+        moved_out[me] = moved_ref[me]
+        for i in range(size - 1):
+            moved_copy(i).wait_recv()
+            moved_out[(me + size - i - 1) % size] = moved_in[i]
+            moved_copy(i).wait_send()
     for step in range(LINE):
         for h in range(HALVES):
             x_copy(step, h).wait_send()
@@ -226,39 +251,54 @@
                 z_copy(step, h).wait_send()
 
 
-def product_scatter(rows, weight, collective_id):
+def product_scatter(rows, weight, collective_id, moved=None):
     size = lax.axis_size("fsdp")
+    exchange = moved is not None
     if size != 2 * LINE:
         part = jnp.dot(rows, weight, preferred_element_type=jnp.float32).astype(jnp.bfloat16)
-        return lax.psum_scatter(part, "fsdp", scatter_dimension=1, tiled=True).astype(jnp.float32)
+        kept = lax.psum_scatter(part, "fsdp", scatter_dimension=1, tiled=True).astype(jnp.float32)
+        if not exchange:
+            return kept
+        return kept, lax.all_to_all(moved, "fsdp", split_axis=0, concat_axis=0, tiled=True)
     count, depth = rows.shape
     width = weight.shape[1] // size
     unit = (HALVES, count, width // HALVES)
-    return pl.pallas_call(
-        product_scatter_kernel,
-        out_shape=jax.ShapeDtypeStruct((count, width), jnp.float32),
-        in_specs=[
-            pl.BlockSpec(memory_space=pltpu.VMEM),
-            pl.BlockSpec(memory_space=pl.ANY),
-        ],
-        out_specs=pl.BlockSpec(memory_space=pltpu.VMEM),
-        scratch_shapes=[
-            pltpu.VMEM((2 * LINE, depth, width), jnp.bfloat16),
-            pltpu.VMEM((LINE,) + unit, jnp.bfloat16),
-            pltpu.VMEM((LINE,) + unit, jnp.bfloat16),
-            pltpu.VMEM((LINE,) + unit, jnp.bfloat16),
-            pltpu.VMEM((LINE - 1,) + unit, jnp.bfloat16),
-            pltpu.VMEM((LINE + 1,) + unit, jnp.bfloat16),
-            pltpu.SemaphoreType.DMA((2 * LINE,)),
-            pltpu.SemaphoreType.DMA((LINE, HALVES)),
-            pltpu.SemaphoreType.DMA((LINE, HALVES)),
-            pltpu.SemaphoreType.DMA((LINE - 1, HALVES)),
-            pltpu.SemaphoreType.DMA((LINE + 1, HALVES)),
-        ],
+    vmem = pl.BlockSpec(memory_space=pltpu.VMEM)
+    operands, in_specs = [rows, weight], [vmem, pl.BlockSpec(memory_space=pl.ANY)]
+    out_shape, out_specs = [jax.ShapeDtypeStruct((count, width), jnp.float32)], [vmem]
+    scratch = [
+        pltpu.VMEM((size, depth, width), jnp.bfloat16),
+        pltpu.VMEM((LINE,) + unit, jnp.bfloat16),
+        pltpu.VMEM((LINE,) + unit, jnp.bfloat16),
+        pltpu.VMEM((LINE,) + unit, jnp.bfloat16),
+        pltpu.VMEM((LINE - 1,) + unit, jnp.bfloat16),
+        pltpu.VMEM((LINE + 1,) + unit, jnp.bfloat16),
+        pltpu.SemaphoreType.DMA((size,)),
+        pltpu.SemaphoreType.DMA((LINE, HALVES)),
+        pltpu.SemaphoreType.DMA((LINE, HALVES)),
+        pltpu.SemaphoreType.DMA((LINE - 1, HALVES)),
+        pltpu.SemaphoreType.DMA((LINE + 1, HALVES)),
+    ]
+    if exchange:
+        operands.append(moved)
+        in_specs.append(vmem)
+        out_shape.append(jax.ShapeDtypeStruct(moved.shape, moved.dtype))
+        out_specs.append(vmem)
+        scratch += [
+            pltpu.VMEM((size - 1,) + moved.shape[1:], moved.dtype),
+            pltpu.SemaphoreType.DMA((size - 1,)),
+            pltpu.SemaphoreType.DMA((size - 1,)),
+        ]
+    results = pl.pallas_call(
+        functools.partial(product_scatter_kernel, exchange),
+        out_shape=out_shape,
+        in_specs=in_specs,
+        out_specs=out_specs,
+        scratch_shapes=scratch,
         compiler_params=pltpu.CompilerParams(
             collective_id=collective_id,
             has_side_effects=True,
-            vmem_limit_bytes=50 * 1024 * 1024,
+            vmem_limit_bytes=52 * 1024 * 1024,
         ),
         cost_estimate=pl.CostEstimate(
             flops=2 * count * depth * width * size,
@@ -266,7 +306,8 @@
             transcendentals=0,
         ),
         name="product_scatter",
-    )(rows, weight)
+    )(*operands)
+    return results if exchange else results[0]
 
 
 def latents_kernel(
@@ -378,7 +419,7 @@
     )(lax.axis_index("img").astype(jnp.int32).reshape(1), cross_key, cross_value)
 
 
-def head_weights(cross_key, cross_value):
+def weight_blocks(cross_key, cross_value):
     fsdp_size, img_size = lax.axis_size("fsdp"), lax.axis_size("img")
     my_shard = lax.axis_index("img")
     rows = cross_key.shape[0]
@@ -389,12 +430,9 @@
         return lax.dynamic_index_in_dim(split, my_shard, 2, keepdims=False)
 
     if part % LANES == 0:
-        both = pick_columns(cross_key, cross_value, fsdp_size, img_size, part)
-    else:
-        both = jnp.concatenate([mine(cross_key), mine(cross_value)], 2)
-        both = jnp.transpose(both, (1, 0, 2))
-    both = lax.all_to_all(both, "fsdp", split_axis=0, concat_axis=0, tiled=True)
-    return lax.all_gather(both.reshape(fsdp_size * rows, 2 * part), "img", axis=0)
+        return pick_columns(cross_key, cross_value, fsdp_size, img_size, part)
+    both = jnp.concatenate([mine(cross_key), mine(cross_value)], 2)
+    return jnp.transpose(both, (1, 0, 2))
 
 
 def local(
@@ -429,7 +467,6 @@
     res_heads = res_cols // RHD
     head_cols = cross_out.shape[0]
     token_count = text_states.shape[0]
-    slot_count = wanted_images.shape[1]
     cross_heads = head_cols // HEAD
     text_f = text_states.astype(jnp.float32)
     full_patches = lax.all_gather(patches, "fsdp", axis=2, tiled=True)
@@ -439,8 +476,13 @@
     stats = jnp.concatenate(
         [jnp.sum(text_f * text_f, -1), gain_rows, jnp.zeros((SPARE_ROWS * LANES,), jnp.float32)]
     ).reshape(-1, LANES)
-    kv_weights = head_weights(cross_key, cross_value)
-    query = product_scatter((text_f * text_gain).astype(jnp.bfloat16), cross_query, 0)
+    query, kv_weights = product_scatter(
+        (text_f * text_gain).astype(jnp.bfloat16),
+        cross_query,
+        0,
+        weight_blocks(cross_key, cross_value),
+    )
+    kv_weights = lax.all_gather(kv_weights.reshape(vis_width, -1), "img", axis=0)
     full_patches, query = lax.optimization_barrier((full_patches, query))
     context = layer_norm(full_patches, context_gain).astype(jnp.bfloat16)
     latent_normed = layer_norm(latent_init, latent_gain).astype(jnp.bfloat16)
@@ -482,23 +524,23 @@
     resampled, sums = normed_latents(mixed_part.astype(jnp.bfloat16), init_rows, stats)
     squares = sums.reshape(-1)[:token_count]
     query = (query * lax.rsqrt(squares / D + eps_rms)[:, None]).astype(jnp.bfloat16)
-    per_image = resampled.reshape(image_count, latent_count * vis_width)
+    per_image = resampled.reshape(image_count, latent_count, vis_width)
     outgoing = pack_rows(per_image, wanted_images, my_shard, image_count, PAIR)
+    outgoing = outgoing.reshape(-1, PAIR * latent_count, vis_width)
     incoming = lax.all_to_all(outgoing, "img", split_axis=0, concat_axis=0, tiled=True)
-    slot_latents = unpack_rows(incoming, wanted_images, my_shard, image_count, PAIR).reshape(
-        slot_count * latent_count, vis_width
-    )
+    slot_latents = incoming.reshape(-1, vis_width)
+    arrived = arrived_slots(wanted_images, my_shard, image_count, PAIR)
     slot_kv = jnp.einsum(
         "lv,ivk->ilk", slot_latents, kv_weights, preferred_element_type=jnp.float32
     ).astype(jnp.bfloat16)
-    slot_kv = slot_kv.reshape(kv_weights.shape[0], slot_count * latent_count, 2, -1)
+    slot_kv = slot_kv.reshape(kv_weights.shape[0], slot_latents.shape[0], 2, -1)
     slot_kv = jnp.transpose(slot_kv, (2, 0, 3, 1)).reshape(2, cross_heads, HEAD, -1)
     slot_keys, slot_values = slot_kv[0], slot_kv[1]
     query_heads = jnp.transpose(query.reshape(token_count, cross_heads, HEAD), (1, 0, 2))
     scores = jnp.einsum(
         "hte,hel->htl", query_heads, slot_keys, preferred_element_type=jnp.float32
     ) * HEAD ** (-0.5)
-    key_slot = jnp.arange(slot_count * latent_count, dtype=jnp.int32) // latent_count
+    key_slot = jnp.repeat(arrived.reshape(-1), latent_count)
     slot_hot = (token_slot[0][:, None] == key_slot[None, :]).astype(jnp.float32)
     weights = jnp.exp(scores) * slot_hot[None]
     weights = (weights / jnp.sum(weights, axis=2, keepdims=True)).astype(jnp.bfloat16)

time: 369 us -> 341 us (0.924)
  blocking collectives: 61.9 us -> 0 us
  Pallas kernels: 229 us -> 271 us
  matrix products: 24.4 us -> 17.6 us
    all_to_all x1 -> x0, blocking collectives: 61.9 us -> none  [head_weights(): both = lax.all_to_all(both, 'fsdp', split_axis=0, concat_axis=0, tiled=True)]
    pallas_call x2, Pallas kernels: 192 us -> 234 us  [product_scatter(): pl.pallas_call(functools.partial(product_scatter_kernel, exchange), out_s...]
    dot_general x2 -> x0, matrix products: 5.55 us -> none  [the longest x1 3.89 us: unpack_rows(): jnp.einsum('cop,opf->cf', taker, received, preferred_element_type=jnp.flo...]
    reshape x3 -> x1, local copies, waits for them, and re-layouts: 4.54 us -> 0.22 us  [local(): slot_kv = slot_kv.reshape(kv_weights.shape[0], slot_latents.shape[0], 2, -1)]
  transfers between devices with their start and end apart: 3 -> 3, of which waited for: 1 -> 1; matrix products, arithmetic and copies ran while one was open for 7% -> 4% of each run, Pallas kernels for 35% -> 51%
where the time goes in v1:
time: 341 us; the launch traced here: 340 us
  Pallas kernels  271 us (79%)
  matrix products  17.6 us (5%)
  waiting for transfers between devices  16.5 us (5%)
  between operations  14.6 us (4%)
  other arithmetic  8.92 us (3%)
  local copies, waits for them, and re-layouts  6.5 us (2%)
  starting transfers between devices  4.57 us (1%)
    pallas_call x2, Pallas kernels, product_scatter(): pl.pallas_call(functools.partial(product_scatter_kernel, exchange), out_s...  234 us
    pallas_call x1, Pallas kernels, normed_latents(): pl.pallas_call(latents_kernel, out_shape=(jax.ShapeDtypeStruct(part.shape...  32 us
    all_to_all x1, waiting for transfers between devices, local(): lax.all_to_all(outgoing, 'img', split_axis=0, concat_axis=0, tiled=True)  15.8 us
  transfers between devices with their start and end apart: 3, of which 1 were waited for; matrix products, arithmetic and copies ran while one was open for 4% of the time, Pallas kernels for 51%

profile of v1, /device:TPU:0, one launch (start us, length us, event | category | flops | bytes accessed | tf_op | source)
XLA Modules:
  0.0 340.0 jit_solution(16783286412758962473)
XLA Ops:
  6.5 0.7 all-gather.5.cloned.1.call-update
  7.3 0.0 all-gather.3.cloned.1.call-start
  7.3 5.5 %pick_columns.1.refs_2_ = bf16[8,160,512]{2,1,0:T(8,128)(2,1)} custom-call(s32[1]{0:T(128)} %bitcast.shard_ref, bf16[160,8192]{1,0:T(8,128)(2,1)} %key_ref.1, bf16[160,8192]{1,0:T(8,128)(2,1)} %value_ref.1), custom_call_target="tpu_custom_call" | custom-call | tf_op jit(solution)/shard_map/pick_columns/pallas_call | solution.py:409
  12.8 0.4 fusion.7
  13.2 136.2 %product_scatter.2 = (f32[512,1024]{1,0:T(8,128)}, bf16[8,160,512]{2,1,0:T(8,128)(2,1)}) custom-call(bf16[512,1024]{1,0:T(8,128)(2,1)S(1)} %get-tuple-element.26.refs_0_, bf16[1024,8192]{1,0:T(8,128)(2,1)} %refs_1_.2, bf16[8,160,512]{2,1,0:T(8,128)(2,1)} %pick_columns.1.refs_2_), custom_call_target="tpu_custom_call" | custom-call | flops 8589934592 | bytes 300000000 | tf_op jit(solution)/shard_map/product_scatter/pallas_call | solution.py:292
  149.4 0.0 all-gather.3.cloned.1.call-update
  149.5 0.1 convert_reduce_fusion.1
  149.7 0.3 convolution_convert_fusion.7
  150.0 0.1 copy.89
  150.1 0.3 convolution_convert_fusion.6
  150.4 0.1 copy.91
  150.6 0.3 convolution_convert_fusion.5
  150.9 0.1 reshape.219
  151.0 0.2 convert_reduce_fusion.2
  151.3 0.1 convolution_convert_fusion.8
  151.4 0.1 fusion.54
  151.5 0.1 copy.100
  151.6 0.1 copy.101
  151.7 0.1 mul.288
  151.8 0.1 mul.289
  151.9 0.1 copy.98
  152.0 0.1 copy.99
  152.1 0.1 mul.280
  152.2 0.1 mul.281
  152.2 0.1 copy.96
  152.4 0.1 copy.97
  152.5 0.1 mul.272
  152.6 0.1 mul.273
  152.6 0.1 copy.86
  152.8 0.1 copy.87
  152.9 0.1 mul.247
  152.9 0.1 mul.248
  153.0 0.2 dynamic_update_slice.3
  153.4 0.0 all-gather.5.cloned.1.call-done
  153.4 2.8 convert_reduce_fusion
  156.3 0.1 copy-done.3
  156.4 1.2 convolution_convert_fusion.3
  157.6 0.1 pad_maximum_fusion
  157.7 1.2 convolution_convert_fusion.2
  158.9 0.1 pad_maximum_fusion.1
  159.0 1.1 divide_convert_fusion.4
  160.1 1.4 fusion.11
  161.4 0.1 copy.95
  161.6 0.1 reshape.220
  161.7 0.3 convolution_convert_fusion.part_ref
  162.1 32.0 %normed_latents.1 = (bf16[256,1280]{1,0:T(8,128)(2,1)S(1)}, f32[16,128]{1,0:T(8,128)S(1)}) custom-call(bf16[256,1280]{1,0:T(8,128)(2,1)S(1)} %convolution_convert_fusion.part_ref, f32[32,1280]{1,0:T(8,128)S(1)} %dynamic-slice_convert_fusion.init_ref, f32[16,128]{1,0:T(8,128)S(1)} %maximum_bitcast_fusion.stats_ref), custom_call_target="tpu_custom_call" | custom-call | flops 6553600 | bytes 100000000 | tf_op jit(solution)/shard_map/normed_latents/pallas_call | solution.py:375
  194.3 1.5 multiply_add_fusion
  195.8 4.5 %all-to-all-start = ((bf16[4,128,1280]{2,1,0:T(8,128)(2,1)}), bf16[4,128,1280]{2,1,0:T(8,128)(2,1)}, u32[]{:S(2)}, u32[]{:S(2)}) async-start(bf16[4,128,1280]{2,1,0:T(8,128)(2,1)} %multiply_add_fusion), calls=%async_computation | async-start | bytes 2621440 | tf_op jit(solution)/shard_map/all_to_all | solution.py:530
  200.3 0.1 multiply_reduce_fusion
  200.5 0.1 copy.106
  200.6 0.1 sub.53
  200.7 0.1 broadcast_in_dim.14
  200.7 0.1 eq.120
  201.5 0.1 compare_convert_fusion
  201.7 15.8 %all-to-all-done = bf16[4,128,1280]{2,1,0:T(8,128)(2,1)} async-done(((bf16[4,128,1280]{2,1,0:T(8,128)(2,1)}), bf16[4,128,1280]{2,1,0:T(8,128)(2,1)}, u32[]{:S(2)}, u32[]{:S(2)}) %all-to-all-start) | async-done | bytes 1310752 | tf_op jit(solution)/shard_map/all_to_all | solution.py:530
  217.4 5.8 %convolution_convert_fusion.1 = bf16[4,512,512]{2,1,0:T(8,128)(2,1)S(1)} fusion(bf16[4,1280,512]{2,1,0:T(8,128)(2,1)} %all-gather.3.cloned.1.call-done, bf16[512,1280,1]{1,0,2:T(8,128)(2,1)} %bitcast.19), kind=kOutput, calls=%fused_computation.19 | convolution fusion | flops 2685403136 | bytes 8650752 | tf_op jit(solution)/shard_map/lv,ivk->ilk/dot_general | solution.py:533
  223.3 0.2 copy.140
  223.5 0.1 fusion.52
  223.6 1.4 copy-done.4
  225.1 2.5 fusion
  227.6 3.1 fusion.8
  230.7 1.5 copy.117.refs_0_
  232.2 97.6 %product_scatter.3 = f32[512,1024]{1,0:T(8,128)} custom-call(bf16[512,1024]{1,0:T(8,128)(2,1)S(1)} %copy.117.refs_0_, bf16[1024,8192]{1,0:T(8,128)(2,1)} %refs_1_.3), custom_call_target="tpu_custom_call" | custom-call | flops 8589934592 | bytes 300000000 | tf_op jit(solution)/shard_map/product_scatter/pallas_call | solution.py:292
  329.8 3.3 convert_add_fusion
  (57 shorter events, 0.4 us)
Async XLA Ops:
  6.5 155.2 %copy-start = (bf16[192,1280]{1,0:T(8,128)(2,1)S(1)}, bf16[192,1280]{1,0:T(8,128)(2,1)}, u32[]{:S(2)}) copy-start(bf16[192,1280]{1,0:T(8,128)(2,1)} %param.32) | copy-start | bytes 1474564
  6.5 146.9 %all-gather.5.cloned.1.call-start = ((), (), s32[]{:S(2)}) async-start(), calls=%async_computation.2 | async-start | bytes 2949120 | tf_op jit(solution)/shard_map/all_gather | solution.py:472
  7.3 210.2 %all-gather.3.cloned.1.call-start = ((), (), s32[]{:S(2)}) async-start(), calls=%async_computation.1 | async-start | bytes 6553600 | tf_op jit(solution)/shard_map/all_gather | solution.py:485
  7.3 5.5 %copy-start.2 = (bf16[512,1024]{1,0:T(8,128)(2,1)S(1)}, bf16[512,1024]{1,0:T(8,128)(2,1)}, u32[]{:S(2)}) copy-start(bf16[512,1024]{1,0:T(8,128)(2,1)} %param.19) | copy-start | bytes 3145732
  7.3 5.5 %copy-start.7 = (f32[1024]{0:T(1024)S(1)}, f32[1024]{0:T(1024)}, u32[]{:S(2)}) copy-start(f32[1024]{0:T(1024)} %param.20) | copy-start | bytes 12292
  13.2 136.3 %copy-start.5 = (bf16[64,1280]{1,0:T(8,128)(2,1)S(1)}, bf16[64,1280]{1,0:T(8,128)(2,1)}, u32[]{:S(2)}) copy-start(bf16[64,1280]{1,0:T(8,128)(2,1)} %param.26) | copy-start | bytes 491524
  13.2 136.5 %copy-start.12 = (bf16[1280,192]{0,1:T(8,128)(2,1)S(1)}, bf16[1280,192]{0,1:T(8,128)(2,1)}, u32[]{:S(2)}) copy-start(bf16[1280,192]{0,1:T(8,128)(2,1)} %param.31) | copy-start | bytes 1474564
  13.2 136.5 %copy-start.14 = (f32[1280]{0:T(1024)S(1)}, f32[1280]{0:T(1024)}, u32[]{:S(2)}) copy-start(f32[1280]{0:T(1024)} %param.28) | copy-start | bytes 15364
  13.2 136.9 %copy-start.13 = (bf16[1280,192]{0,1:T(8,128)(2,1)S(1)}, bf16[1280,192]{0,1:T(8,128)(2,1)}, u32[]{:S(2)}) copy-start(bf16[1280,192]{0,1:T(8,128)(2,1)} %param.30) | copy-start | bytes 1474564
  149.4 1.2 copy-start.11
  149.4 1.6 copy-start.6
  149.4 3.6 %copy-start.10 = (f32[160]{0:T(256)S(1)}, f32[160]{0:T(256)}, u32[]{:S(2)}) copy-start(f32[160]{0:T(256)} %param.33) | copy-start | bytes 1924
  149.7 6.6 %copy-start.15 = (f32[1280]{0:T(1024)S(1)}, f32[1280]{0:T(1024)}, u32[]{:S(2)}) copy-start(f32[1280]{0:T(1024)} %param.27) | copy-start | bytes 15364
  153.4 3.0 copy-start.3
  194.2 7.2 %copy-start.8 = (f32[1024]{0:T(1024)S(1)}, f32[1024]{0:T(1024)}, u32[]{:S(2)}) copy-start(f32[1024]{0:T(1024)} %param.21) | copy-start | bytes 12292
  194.3 7.3 %copy-start.9 = (s32[1,512]{1,0:T(1,128)S(1)}, s32[1,512]{1,0:T(1,128)}, u32[]{:S(2)}) copy-start(s32[1,512]{1,0:T(1,128)} %param.23) | copy-start | bytes 6148
  195.8 21.6 %all-to-all-start = ((bf16[4,128,1280]{2,1,0:T(8,128)(2,1)}), bf16[4,128,1280]{2,1,0:T(8,128)(2,1)}, u32[]{:S(2)}, u32[]{:S(2)}) async-start(bf16[4,128,1280]{2,1,0:T(8,128)(2,1)} %multiply_add_fusion), calls=%async_computation | async-start | bytes 2621440 | tf_op jit(solution)/shard_map/all_to_all | solution.py:530
  223.5 1.6 copy-start.4
  232.2 100.9 %copy-start.1 = (bf16[192,1280]{1,0:T(8,128)(2,1)S(1)}, bf16[192,1280]{1,0:T(8,128)(2,1)}, u32[]{:S(2)}) copy-start(bf16[192,1280]{1,0:T(8,128)(2,1)} %param.32) | copy-start | bytes 1474564
Sparse Core Ops, SparseCore 0:
  9.6 92.6 all-gather.4
  149.6 39.6 all-gather.2
